TPU v7x, 32 devices: a whole 2x2x4 slice. The times are simulated.
32 devices in a mesh: elec: 8 (over z, y), space: 4 (over x, core).
Axes of the slice: x: 2, y: 2, z: 4, core: 2. Of those that a mesh axis runs over, the one named last changes fastest.
Arguments:
- sigma_real: float32 [8, 64, 128], P('space'), may hold values from 0.3 to 3
- sigma_imag: float32 [8, 64, 128], P('space'), may hold values from -0.5 to 0.5
- warm_fields: float32 [32, 2, 8, 64, 128], P('elec', None, 'space'), may hold values from -6 to 6
- locations: int32 [32], P('elec'), may hold values from 0 to 65535
- counts: int32 [8], P('elec'), may hold values from 1 to 48, 128 in all
- quads: int32 [8, 48, 4], P('elec'), may hold values from 0 to 31
Outputs:
- jacobian: bfloat16 [128, 2, 8, 64, 128], P('elec', None, 'space')
Inputs may be any that keep to these rules, and one draw needn't show every extreme that they name: The counts sum to 128; group h's measurements are its first counts[h] slots. `quads`: slots past a group's count are unused.
All inputs are finite; a program needn't handle non-finite values.
Results may differ from a plain program's by a relative error of at most 0.0072.
Values may be sent and summed in bfloat16 or wider, within the bound.
A program may use at most 128 MiB of HBM per device.

v0:
```python
import math
import jax
import jax.numpy as jnp
from jax import lax
from jax.sharding import PartitionSpec as P

MEASURE_ROWS_MEAN = 16
ITERS = 2
screen = 0.3
current = 4.0


def padded_2(cells, sides, width):
    for axis, dim in sides:
        count = lax.axis_size(axis)
        ends = count - 1
        head = lax.slice_in_dim(cells, 0, width, axis=dim)
        tail = lax.slice_in_dim(cells, cells.shape[dim] - width, cells.shape[dim], axis=dim)
        cells = jnp.concatenate(
            [
                lax.ppermute(tail, axis, [(i, (i + 1) % count) for i in range(ends)]),
                cells,
                lax.ppermute(head, axis, [((i + 1) % count, i) for i in range(ends)]),
            ],
            axis=dim,
        )
    return cells


def relax_weights(count):
    spread_half = 6.0 / (6.0 + screen)
    return [
        1.0 / (1.0 + spread_half * math.cos(math.pi * (2 * k + 1) / (2 * count)))
        for k in range(count)
    ]


def gradients_of(padded_potential):
    values = padded_potential.astype(jnp.float32)
    interior = values[:, :, 1:-1]
    grad_x = (values[:, :, 2:] - values[:, :, :-2]) * 0.5
    side_pad = jnp.pad(interior, ((0, 0), (0, 0), (0, 0), (1, 1), (1, 1)))
    grad_y = (side_pad[:, :, :, 2:, 1:-1] - side_pad[:, :, :, :-2, 1:-1]) * 0.5
    grad_z = (side_pad[:, :, :, 1:-1, 2:] - side_pad[:, :, :, 1:-1, :-2]) * 0.5
    return jnp.stack([grad_x, grad_y, grad_z], axis=2).astype(jnp.bfloat16)


def per_device(sigma_real, sigma_imag, warm_fields, locations, counts, quads):
    group_width, cells_along_y, cells_along_z = sigma_real.shape
    slab = lax.axis_index("space")
    x_global = slab * group_width + lax.broadcasted_iota(
        jnp.int32, (group_width, cells_along_y, cells_along_z), 0
    )
    y_index = lax.broadcasted_iota(jnp.int32, (group_width, cells_along_y, cells_along_z), 1)
    z_index = lax.broadcasted_iota(jnp.int32, (group_width, cells_along_y, cells_along_z), 2)
    flat_index = (x_global * cells_along_y + y_index) * cells_along_z + z_index
    inverse = 1.0 / ((6.0 + screen) * (sigma_real * sigma_real + sigma_imag * sigma_imag))
    strength = jnp.where(
        flat_index[None] == locations[:, None, None, None], jnp.float32(current), jnp.float32(0.0)
    )
    source = jnp.stack(
        [strength * sigma_real * inverse, -(strength * sigma_imag * inverse)], axis=1
    )
    weights = relax_weights(ITERS)
    field = warm_fields
    for iteration in range(ITERS):
        padded = padded_2(field, (("space", 2),), 1)
        interior = padded[:, :, 1:-1]
        side_pad = jnp.pad(interior, ((0, 0), (0, 0), (0, 0), (1, 1), (1, 1)))
        total = padded[:, :, 2:] + padded[:, :, :-2]
        total = total + side_pad[:, :, :, 2:, 1:-1] + side_pad[:, :, :, :-2, 1:-1]
        total = total + side_pad[:, :, :, 1:-1, 2:] + side_pad[:, :, :, 1:-1, :-2]
        field = field + weights[iteration] * (source - field + total / (6.0 + screen))
    potential = field.astype(jnp.bfloat16)
    own_grads = gradients_of(padded_2(potential, (("space", 2),), 1))
    gradient_table = lax.all_gather(own_grads, "elec", axis=0, tiled=True)
    all_counts, all_quads = (
        lax.all_gather(counts, "elec", axis=0, tiled=True),
        lax.all_gather(quads, "elec", axis=0, tiled=True),
    )
    capacity = all_quads.shape[1]
    ends = jnp.cumsum(all_counts)
    starts = ends - all_counts
    measure_group = lax.axis_index("elec")
    row_indices = measure_group * MEASURE_ROWS_MEAN + jnp.arange(MEASURE_ROWS_MEAN, dtype=jnp.int32)
    owners = jnp.sum((ends[None, :] <= row_indices[:, None]).astype(jnp.int32), axis=1)
    slot_ids = row_indices - starts[owners]
    chosen = all_quads.reshape(-1, 4)[owners * capacity + slot_ids]
    electrodes = gradient_table.shape[0]
    electrode_ids = jnp.arange(electrodes, dtype=jnp.int32)[None, :]
    select_source = (chosen[:, 0:1] == electrode_ids).astype(jnp.float32) - (
        chosen[:, 1:2] == electrode_ids
    ).astype(jnp.float32)
    select_probe = (chosen[:, 2:3] == electrode_ids).astype(jnp.float32) - (
        chosen[:, 3:4] == electrode_ids
    ).astype(jnp.float32)
    selector = jnp.concatenate([select_source, select_probe], axis=0).astype(jnp.bfloat16)
    field_products = jnp.dot(
        selector, gradient_table.reshape(electrodes, -1), preferred_element_type=jnp.float32
    )
    field_products = field_products.reshape(
        2, MEASURE_ROWS_MEAN, 2, 3, group_width, cells_along_y, cells_along_z
    )
    pair_source = field_products[0]
    pair_probe = field_products[1]
    dot_real = jnp.sum(
        pair_source[:, 0] * pair_probe[:, 0] - pair_source[:, 1] * pair_probe[:, 1], axis=1
    )
    dot_imag = jnp.sum(
        pair_source[:, 0] * pair_probe[:, 1] + pair_source[:, 1] * pair_probe[:, 0], axis=1
    )
    part_real = -(sigma_real * dot_real - sigma_imag * dot_imag)
    part_imag = -(sigma_real * dot_imag + sigma_imag * dot_real)
    return jnp.stack([part_real, part_imag], axis=1).astype(jnp.bfloat16)


def solution(mesh):
    in_specs = (
        P("space", None, None),
        P("space", None, None),
        P("elec", None, "space", None, None),
        P("elec"),
        P("elec"),
        P("elec", None, None),
    )
    out_specs = P("elec", None, "space", None, None)
    return jax.shard_map(
        per_device, mesh=mesh, in_specs=in_specs, out_specs=out_specs, check_vma=False
    )
```

profile of v0, /device:TPU:0, one launch (start us, length us, event | category | flops | bytes accessed | tf_op | source)
XLA Modules:
  0.0 178.6 jit_solution(6735330070216509067)
XLA Ops:
  6.5 0.0 all-gather.2.cloned.1.call-start
  6.5 1.1 fusion.50
  7.6 1.3 collective-permute-start
  8.9 3.0 %collective-permute-start.1 = (f32[4,2,1,64,128]{4,3,2,1,0:T(8,128)S(1)}, f32[4,2,1,64,128]{4,3,2,1,0:T(8,128)S(1)}, u32[]{:S(2)}, u32[]{:S(2)}) collective-permute-start(f32[4,2,1,64,128]{4,3,2,1,0:T(8,128)S(1)} %get-tuple-element.22), channel_id=1, source_target_pairs={{0,1},{1,2},{2,3},{4,5},{5,6},{6,7},{8,9},{9,10},{10,11},{12,13},{... | collective-permute-start | bytes 786440 | tf_op jit(solution)/shard_map/ppermute | solution.py:21
  12.0 0.9 multiply_divide_fusion
  12.9 0.1 iota_add_fusion
  13.0 1.0 fusion.36
  14.0 0.0 collective-permute-done
  14.0 0.0 collective-permute-done.1
  14.0 0.0 copy-start.3
  14.0 0.0 copy-start.2
  14.0 3.0 %fusion.16 = f32[4,2,2,64,128]{4,3,2,1,0:T(8,128)S(1)} fusion(f32[4,2,2,64,128]{4,3,2,1,0:T(8,128)} %param.8, f32[4,2,1,64,128]{4,3,2,1,0:T(8,128)S(1)} %collective-permute-done.1, f32[4,2,1,64,128]{4,3,2,1,0:T(8,128)S(1)} %collective-permute-done, f32[4,1,2,64,128]{4,3,2,1,0:T(8,128)S(1)} %get-tuple-element.26, f32[4,1,2,64,128]{4,3,2,1,0:T(8,128)S(1)} %get-tuple-element.25), kind=kLoop, calls=%fused_computation.40 | loop fusion | flops 1703936 | bytes 2097152 | tf_op jit(solution)/shard_map/add | solution.py:73
  17.1 1.3 collective-permute-start.2
  18.4 6.3 %collective-permute-start.3 = (f32[4,2,1,64,128]{4,3,2,1,0:T(8,128)S(1)}, f32[4,2,1,64,128]{4,3,2,1,0:T(8,128)S(1)}, u32[]{:S(2)}, u32[]{:S(2)}) collective-permute-start(f32[4,2,1,64,128]{4,3,2,1,0:T(8,128)S(1)} %get-tuple-element.20), channel_id=1, source_target_pairs={{0,1},{1,2},{2,3},{4,5},{5,6},{6,7},{8,9},{9,10},{10,11},{12,13},{... | collective-permute-start | bytes 786440 | tf_op jit(solution)/shard_map/ppermute | solution.py:21
  24.7 0.0 collective-permute-done.2
  24.8 1.1 collective-permute-done.3
  25.9 0.5 fusion.25
  26.4 6.5 %collective-permute-start.4 = (bf16[4,2,1,64,128]{4,3,2,1,0:T(8,128)(2,1)S(1)}, bf16[4,2,1,64,128]{4,3,2,1,0:T(8,128)(2,1)S(1)}, u32[]{:S(2)}, u32[]{:S(2)}) collective-permute-start(bf16[4,2,1,64,128]{4,3,2,1,0:T(8,128)(2,1)S(1)} %get-tuple-element.23), channel_id=1, source_target_pairs={{0,1},{1,2},{2,3},{4,5},{5,6},{6,7},{8,9},{9,10},{10,11},{12,13},{... | collective-permute-start | bytes 393224 | tf_op jit(solution)/shard_map/ppermute | solution.py:21
  32.9 1.3 collective-permute-start.5
  34.2 0.0 collective-permute-done.4
  34.2 3.9 %collective-permute-done.5 = bf16[4,2,1,64,128]{4,3,2,1,0:T(8,128)(2,1)S(1)} collective-permute-done((bf16[4,2,1,64,128]{4,3,2,1,0:T(8,128)(2,1)S(1)}, bf16[4,2,1,64,128]{4,3,2,1,0:T(8,128)(2,1)S(1)}, u32[]{:S(2)}, u32[]{:S(2)}) %collective-permute-start.5) | collective-permute-done | bytes 131104 | tf_op jit(solution)/shard_map/ppermute | solution.py:23
  38.1 0.1 maximum_convert_fusion
  38.2 0.1 fusion.39
  38.3 0.4 fusion.41
  38.7 1.0 pad_maximum_fusion.1
  39.7 0.0 all-gather.2.cloned.1.call-update
  40.4 0.0 copy-done.3
  40.4 0.6 dynamic-slice
  41.0 0.7 dynamic-update-slice
  41.7 11.6 %all-reduce.3 = s32[8]{0:T(128)S(1)} all-reduce(s32[8]{0:T(128)S(1)} %dynamic-update-slice), channel_id=1, replica_groups=mesh['elec'=8,'space'=4] {'elec'}, use_global_device_ids=true, to_apply=%add.3 | all-reduce | flops 8 | bytes 64
  53.3 0.2 reduce-window.8
  53.5 0.0 copy-done.2
  53.5 26.8 %all_gather.9 = s32[8,48,4]{1,2,0:T(4,128)S(1)} all-gather(s32[1,48,4]{1,2,0:T(4,128)S(1)} %copy-done.2), channel_id=1, replica_groups=mesh['elec'=8,'space'=4] {'elec'}, dimensions={0}, use_global_device_ids=true | all-gather | bytes 6912 | tf_op jit(solution)/shard_map/all_gather | solution.py:79
  80.2 0.1 copy.12
  80.4 0.1 convert_reduce_fusion
  80.5 0.7 gather_fusion
  81.2 0.6 gather_fusion.1
  81.7 0.2 slice_reduce_fusion.3
  81.9 0.1 subtract_convert_fusion
  82.0 60.7 %all-gather.2.cloned.1.call-done = bf16[32,2,3,2,64,128]{5,4,3,1,0,2:T(8,128)(2,1)} async-done(((bf16[4,2,3,2,64,128]{5,4,3,1,0,2:T(8,128)(2,1)}), bf16[32,2,3,2,64,128]{5,4,3,1,0,2:T(8,128)(2,1)}) %all-gather.2.cloned.1.call-update) | async-done | bytes 6291472 | tf_op jit(solution)/shard_map/all_gather | solution.py:76
  142.7 4.3 %copy.13 = bf16[32,2,3,2,64,128]{5,4,3,2,1,0:T(8,128)(2,1)S(1)} copy(bf16[32,2,3,2,64,128]{5,4,3,1,0,2:T(8,128)(2,1)} %all-gather.2.cloned.1.call-done) | data formatting | bytes 12582912 | tf_op jit(solution)/shard_map/all_gather | solution.py:76
  147.0 8.3 %fusion = f32[32,98304]{1,0:T(8,128)} fusion(bf16[4,8,768,128]{3,2,1,0:T(8,128)(2,1)S(1)} %bitcast.61, bf16[16,32]{1,0:T(8,128)(2,1)S(1)} %get-tuple-element.27, bf16[16,32]{1,0:T(8,128)(2,1)S(1)} %get-tuple-element.28), kind=kOutput, calls=%fused_computation.2 | convolution fusion | flops 201330688 | bytes 18876416 | tf_op jit(solution)/shard_map/dot_general | solution.py:98
  155.3 8.0 %slice_bitcast_fusion.1 = (f32[2,8,768,128]{3,1,2,0:T(8,128)}, f32[2,8,768,128]{3,1,2,0:T(8,128)S(1)}) fusion(f32[32,98304]{1,0:T(8,128)} %fusion), kind=kLoop, calls=%fused_computation.6 | loop fusion | bytes 25165824
  163.4 4.0 %copy.15 = f32[2,8,768,128]{3,2,1,0:T(8,128)S(1)} copy(f32[2,8,768,128]{3,1,2,0:T(8,128)} %get-tuple-element.11) | data formatting | bytes 12582912
  167.4 1.2 copy.16
  168.6 0.0 copy-start
  168.6 0.0 copy-start.1
  168.6 1.7 subtract_reduce_fusion
  170.3 0.0 copy-done
  170.3 0.0 copy-done.1
  170.3 0.4 fusion.5
  170.7 1.1 pad_maximum_fusion
  (10 shorter events, 0.1 us)
Async XLA Ops:
  6.5 136.2 %all-gather.2.cloned.1.call-start = ((), (), s32[]{:S(2)}) async-start(), calls=%async_computation | async-start | bytes 7077888 | tf_op jit(solution)/shard_map/all_gather | solution.py:76
  7.6 6.4 %collective-permute-start = (f32[4,2,1,64,128]{4,3,2,1,0:T(8,128)S(1)}, f32[4,2,1,64,128]{4,3,2,1,0:T(8,128)S(1)}, u32[]{:S(2)}, u32[]{:S(2)}) collective-permute-start(f32[4,2,1,64,128]{4,3,2,1,0:T(8,128)S(1)} %get-tuple-element.21), channel_id=1, source_target_pairs={{1,0},{2,1},{3,2},{5,4},{6,5},{7,6},{9,8},{10,9},{11,10},{13,12},{... | collective-permute-start | bytes 786440 | tf_op jit(solution)/shard_map/ppermute | solution.py:23
  8.9 5.1 %collective-permute-start.1 = (f32[4,2,1,64,128]{4,3,2,1,0:T(8,128)S(1)}, f32[4,2,1,64,128]{4,3,2,1,0:T(8,128)S(1)}, u32[]{:S(2)}, u32[]{:S(2)}) collective-permute-start(f32[4,2,1,64,128]{4,3,2,1,0:T(8,128)S(1)} %get-tuple-element.22), channel_id=1, source_target_pairs={{0,1},{1,2},{2,3},{4,5},{5,6},{6,7},{8,9},{9,10},{10,11},{12,13},{... | collective-permute-start | bytes 786440 | tf_op jit(solution)/shard_map/ppermute | solution.py:21
  14.0 26.4 %copy-start.3 = (u32[32]{0:T(128)S(1)}, u32[32]{0:T(128)}, u32[]{:S(2)}) copy-start(u32[32]{0:T(128)} %constant.62) | copy-start | bytes 388
  14.0 39.4 %copy-start.2 = (s32[1,48,4]{1,2,0:T(4,128)S(1)}, s32[1,48,4]{1,2,0:T(4,128)}, u32[]{:S(2)}) copy-start(s32[1,48,4]{1,2,0:T(4,128)} %param.11) | copy-start | bytes 2308
  17.1 7.6 %collective-permute-start.2 = (f32[4,2,1,64,128]{4,3,2,1,0:T(8,128)S(1)}, f32[4,2,1,64,128]{4,3,2,1,0:T(8,128)S(1)}, u32[]{:S(2)}, u32[]{:S(2)}) collective-permute-start(f32[4,2,1,64,128]{4,3,2,1,0:T(8,128)S(1)} %get-tuple-element.19), channel_id=1, source_target_pairs={{1,0},{2,1},{3,2},{5,4},{6,5},{7,6},{9,8},{10,9},{11,10},{13,12},{... | collective-permute-start | bytes 786440 | tf_op jit(solution)/shard_map/ppermute | solution.py:23
  18.4 7.5 %collective-permute-start.3 = (f32[4,2,1,64,128]{4,3,2,1,0:T(8,128)S(1)}, f32[4,2,1,64,128]{4,3,2,1,0:T(8,128)S(1)}, u32[]{:S(2)}, u32[]{:S(2)}) collective-permute-start(f32[4,2,1,64,128]{4,3,2,1,0:T(8,128)S(1)} %get-tuple-element.20), channel_id=1, source_target_pairs={{0,1},{1,2},{2,3},{4,5},{5,6},{6,7},{8,9},{9,10},{10,11},{12,13},{... | collective-permute-start | bytes 786440 | tf_op jit(solution)/shard_map/ppermute | solution.py:21
  26.4 7.9 %collective-permute-start.4 = (bf16[4,2,1,64,128]{4,3,2,1,0:T(8,128)(2,1)S(1)}, bf16[4,2,1,64,128]{4,3,2,1,0:T(8,128)(2,1)S(1)}, u32[]{:S(2)}, u32[]{:S(2)}) collective-permute-start(bf16[4,2,1,64,128]{4,3,2,1,0:T(8,128)(2,1)S(1)} %get-tuple-element.23), channel_id=1, source_target_pairs={{0,1},{1,2},{2,3},{4,5},{5,6},{6,7},{8,9},{9,10},{10,11},{12,13},{... | collective-permute-start | bytes 393224 | tf_op jit(solution)/shard_map/ppermute | solution.py:21
  32.9 5.2 %collective-permute-start.5 = (bf16[4,2,1,64,128]{4,3,2,1,0:T(8,128)(2,1)S(1)}, bf16[4,2,1,64,128]{4,3,2,1,0:T(8,128)(2,1)S(1)}, u32[]{:S(2)}, u32[]{:S(2)}) collective-permute-start(bf16[4,2,1,64,128]{4,3,2,1,0:T(8,128)(2,1)S(1)} %get-tuple-element.24), channel_id=1, source_target_pairs={{1,0},{2,1},{3,2},{5,4},{6,5},{7,6},{9,8},{10,9},{11,10},{13,12},{... | collective-permute-start | bytes 393224 | tf_op jit(solution)/shard_map/ppermute | solution.py:23
  168.6 1.7 copy-start
  168.6 1.7 copy-start.1
Sparse Core Ops, SparseCore 0:
  39.8 102.8 all-gather.1
where the time goes:
time: 179 us
  waiting for transfers between devices  65.8 us (37%)
  blocking collectives  38.4 us (21%)
  local copies, waits for them, and re-layouts  21.5 us (12%)
  starting transfers between devices  19.8 us (11%)
  between operations  14.3 us (8%)
  other arithmetic  10.5 us (6%)
  matrix products  8.32 us (5%)
    all_gather x1, waiting for transfers between devices, per_device(): gradient_table = lax.all_gather(own_grads, 'elec', axis=0, tiled=True)  60.7 us
    all_gather x1, blocking collectives, per_device(): lax.all_gather(quads, 'elec', axis=0, tiled=True)  26.8 us
    ppermute x3, starting transfers between devices, padded_2(): lax.ppermute(tail, axis, [(i, (i + 1) % count) for i in range(ends)])  15.9 us
    unnamed x14, local copies, waits for them, and re-layouts  14.5 us
    unnamed x1, blocking collectives  11.6 us
    dot_general x1, matrix products, per_device(): jnp.dot(selector, gradient_table.reshape(electrodes, -1), preferred_eleme...  8.32 us
    all_gather x1, local copies, waits for them, and re-layouts, per_device(): gradient_table = lax.all_gather(own_grads, 'elec', axis=0, tiled=True)  4.28 us
    ppermute x3, waiting for transfers between devices, padded_2(): lax.ppermute(head, axis, [((i + 1) % count, i) for i in range(ends)])  3.92 us
  transfers between devices with their start and end apart: 7, of which 3 were waited for; matrix products, arithmetic and copies ran while one was open for 3% of the time, Pallas kernels for 0%

commit v1 on v0

--- a/solution.py
+++ b/solution.py
@@ -73,7 +73,12 @@
         field = field + weights[iteration] * (source - field + total / (6.0 + screen))
     potential = field.astype(jnp.bfloat16)
     own_grads = gradients_of(padded_2(potential, (("space", 2),), 1))
-    gradient_table = lax.all_gather(own_grads, "elec", axis=0, tiled=True)
+    ring = [own_grads]
+    for hop in range(7):
+        ring.append(lax.ppermute(ring[-1], "elec", [(dev, (dev + 1) % 8) for dev in range(8)]))
+    gradient_table = jnp.roll(
+        jnp.concatenate(ring[::-1], axis=0), (lax.axis_index("elec") + 1) * ring[0].shape[0], axis=0
+    )
     all_counts, all_quads = (
         lax.all_gather(counts, "elec", axis=0, tiled=True),
         lax.all_gather(quads, "elec", axis=0, tiled=True),

time: 179 us -> 263 us (1.47)
  waiting for transfers between devices: 65.8 us -> 124 us
  local copies, waits for them, and re-layouts: 21.5 us -> 49 us
  between operations: 14.3 us -> 0.98 us
  blocking collectives: 38.4 us -> 45 us
  starting transfers between devices: 19.8 us -> 23.6 us
    ppermute x0 -> x7, waiting for transfers between devices: none -> 119 us  [per_device(): lax.ppermute(ring[-1], 'elec', [(dev, (dev + 1) % 8) for dev in range(8)])]
    all_gather x1 -> x0, waiting for transfers between devices: 60.7 us -> none  [per_device(): gradient_table = lax.all_gather(own_grads, 'elec', axis=0, tiled=True)]
    unnamed x14 -> x28, local copies, waits for them, and re-layouts: 14.5 us -> 39.1 us
    dynamic_slice x0 -> x2, local copies, waits for them, and re-layouts: none -> 7.17 us  [per_device(): jnp.roll(jnp.concatenate(ring[::-1], axis=0), (lax.axis_index('elec') + 1...]
    all_gather x1 -> x0, local copies, waits for them, and re-layouts: 4.28 us -> none  [per_device(): gradient_table = lax.all_gather(own_grads, 'elec', axis=0, tiled=True)]
    all_gather x1, blocking collectives: 26.8 us -> 30.8 us  [per_device(): lax.all_gather(quads, 'elec', axis=0, tiled=True)]
    ppermute x0 -> x7, starting transfers between devices: none -> 3.83 us  [per_device(): lax.ppermute(ring[-1], 'elec', [(dev, (dev + 1) % 8) for dev in range(8)])]
  transfers between devices with their start and end apart: 7 -> 13, of which waited for: 3 -> 8; matrix products, arithmetic and copies ran while one was open for 3% -> 2% of each run, Pallas kernels for 0% -> 0%
where the time goes in v1:
time: 263 us; the launch traced here: 262 us
  waiting for transfers between devices  124 us (47%)
  local copies, waits for them, and re-layouts  49 us (19%)
  blocking collectives  45 us (17%)
  starting transfers between devices  23.6 us (9%)
  other arithmetic  11.7 us (4%)
  matrix products  8.32 us (3%)
    ppermute x7, waiting for transfers between devices, per_device(): lax.ppermute(ring[-1], 'elec', [(dev, (dev + 1) % 8) for dev in range(8)])  119 us
    unnamed x28, local copies, waits for them, and re-layouts  39.1 us
    all_gather x1, blocking collectives, per_device(): lax.all_gather(quads, 'elec', axis=0, tiled=True)  30.8 us
    ppermute x3, starting transfers between devices, padded_2(): lax.ppermute(tail, axis, [(i, (i + 1) % count) for i in range(ends)])  15.9 us
    unnamed x1, blocking collectives  14.2 us
    dot_general x1, matrix products, per_device(): jnp.dot(selector, gradient_table.reshape(electrodes, -1), preferred_eleme...  8.32 us
    dynamic_slice x2, local copies, waits for them, and re-layouts, per_device(): jnp.roll(jnp.concatenate(ring[::-1], axis=0), (lax.axis_index('elec') + 1...  7.17 us
  transfers between devices with their start and end apart: 13, of which 8 were waited for; matrix products, arithmetic and copies ran while one was open for 2% of the time, Pallas kernels for 0%

profile of v1, /device:TPU:0, one launch (start us, length us, event | category | flops | bytes accessed | tf_op | source)
XLA Modules:
  0.0 262.4 jit_solution(2402827462591655856)
XLA Ops:
  0.0 1.1 fusion.50
  1.1 1.3 collective-permute-start
  2.4 3.0 %collective-permute-start.1 = (f32[4,2,1,64,128]{4,3,2,1,0:T(8,128)S(1)}, f32[4,2,1,64,128]{4,3,2,1,0:T(8,128)S(1)}, u32[]{:S(2)}, u32[]{:S(2)}) collective-permute-start(f32[4,2,1,64,128]{4,3,2,1,0:T(8,128)S(1)} %get-tuple-element.22), channel_id=1, source_target_pairs={{0,1},{1,2},{2,3},{4,5},{5,6},{6,7},{8,9},{9,10},{10,11},{12,13},{... | collective-permute-start | bytes 786440 | tf_op jit(solution)/shard_map/ppermute | solution.py:21
  5.5 0.9 multiply_divide_fusion
  6.4 0.1 iota_add_fusion
  6.4 1.0 fusion.36
  7.5 3.0 %fusion.16 = f32[4,2,2,64,128]{4,3,2,1,0:T(8,128)S(1)} fusion(f32[4,2,2,64,128]{4,3,2,1,0:T(8,128)} %param.8, f32[4,2,1,64,128]{4,3,2,1,0:T(8,128)S(1)} %collective-permute-done.1, f32[4,2,1,64,128]{4,3,2,1,0:T(8,128)S(1)} %collective-permute-done, f32[4,1,2,64,128]{4,3,2,1,0:T(8,128)S(1)} %get-tuple-element.26, f32[4,1,2,64,128]{4,3,2,1,0:T(8,128)S(1)} %get-tuple-element.25), kind=kLoop, calls=%fused_computation.40 | loop fusion | flops 1703936 | bytes 2097152 | tf_op jit(solution)/shard_map/add | solution.py:73
  10.6 1.3 collective-permute-start.2
  11.9 6.3 %collective-permute-start.3 = (f32[4,2,1,64,128]{4,3,2,1,0:T(8,128)S(1)}, f32[4,2,1,64,128]{4,3,2,1,0:T(8,128)S(1)}, u32[]{:S(2)}, u32[]{:S(2)}) collective-permute-start(f32[4,2,1,64,128]{4,3,2,1,0:T(8,128)S(1)} %get-tuple-element.20), channel_id=1, source_target_pairs={{0,1},{1,2},{2,3},{4,5},{5,6},{6,7},{8,9},{9,10},{10,11},{12,13},{... | collective-permute-start | bytes 786440 | tf_op jit(solution)/shard_map/ppermute | solution.py:21
  18.2 1.1 collective-permute-done.3
  19.4 0.5 fusion.25
  19.8 6.5 %collective-permute-start.4 = (bf16[4,2,1,64,128]{4,3,2,1,0:T(8,128)(2,1)S(1)}, bf16[4,2,1,64,128]{4,3,2,1,0:T(8,128)(2,1)S(1)}, u32[]{:S(2)}, u32[]{:S(2)}) collective-permute-start(bf16[4,2,1,64,128]{4,3,2,1,0:T(8,128)(2,1)S(1)} %get-tuple-element.23), channel_id=1, source_target_pairs={{0,1},{1,2},{2,3},{4,5},{5,6},{6,7},{8,9},{9,10},{10,11},{12,13},{... | collective-permute-start | bytes 393224 | tf_op jit(solution)/shard_map/ppermute | solution.py:21
  26.4 1.3 collective-permute-start.5
  27.7 3.9 %collective-permute-done.5 = bf16[4,2,1,64,128]{4,3,2,1,0:T(8,128)(2,1)S(1)} collective-permute-done((bf16[4,2,1,64,128]{4,3,2,1,0:T(8,128)(2,1)S(1)}, bf16[4,2,1,64,128]{4,3,2,1,0:T(8,128)(2,1)S(1)}, u32[]{:S(2)}, u32[]{:S(2)}) %collective-permute-start.5) | collective-permute-done | bytes 131104 | tf_op jit(solution)/shard_map/ppermute | solution.py:23
  31.6 0.1 maximum_convert_fusion
  31.7 0.1 fusion.39
  31.8 0.4 fusion.41
  32.2 0.1 pad_maximum_fusion.1
  32.3 1.6 collective-permute-start.6
  33.9 18.8 %collective-permute-done.6 = bf16[4,2,3,2,64,128]{5,4,3,1,0,2:T(8,128)(2,1)S(1)} collective-permute-done((bf16[4,2,3,2,64,128]{5,4,3,1,0,2:T(8,128)(2,1)S(1)}, bf16[4,2,3,2,64,128]{5,4,3,1,0,2:T(8,128)(2,1)S(1)}, u32[]{:S(2)}, u32[]{:S(2)}) %collective-permute-start.6) | collective-permute-done | bytes 786464 | tf_op jit(solution)/shard_map/ppermute | solution.py:78
  52.7 21.4 %collective-permute-done.7 = bf16[4,2,3,2,64,128]{5,4,3,1,0,2:T(8,128)(2,1)S(1)} collective-permute-done((bf16[4,2,3,2,64,128]{5,4,3,1,0,2:T(8,128)(2,1)S(1)}, bf16[4,2,3,2,64,128]{5,4,3,1,0,2:T(8,128)(2,1)S(1)}, u32[]{:S(2)}, u32[]{:S(2)}) %collective-permute-start.7) | collective-permute-done | bytes 786464 | tf_op jit(solution)/shard_map/ppermute | solution.py:78
  74.2 22.6 %collective-permute-done.8 = bf16[4,2,3,2,64,128]{5,4,3,1,0,2:T(8,128)(2,1)S(1)} collective-permute-done((bf16[4,2,3,2,64,128]{5,4,3,1,0,2:T(8,128)(2,1)S(1)}, bf16[4,2,3,2,64,128]{5,4,3,1,0,2:T(8,128)(2,1)S(1)}, u32[]{:S(2)}, u32[]{:S(2)}) %collective-permute-start.8) | collective-permute-done | bytes 786464 | tf_op jit(solution)/shard_map/ppermute | solution.py:78
  96.8 22.5 %collective-permute-done.9 = bf16[4,2,3,2,64,128]{5,4,3,1,0,2:T(8,128)(2,1)} collective-permute-done((bf16[4,2,3,2,64,128]{5,4,3,1,0,2:T(8,128)(2,1)S(1)}, bf16[4,2,3,2,64,128]{5,4,3,1,0,2:T(8,128)(2,1)}, u32[]{:S(2)}, u32[]{:S(2)}) %collective-permute-start.9) | collective-permute-done | bytes 786464 | tf_op jit(solution)/shard_map/ppermute | solution.py:78
  119.3 21.9 %collective-permute-done.10 = bf16[4,2,3,2,64,128]{5,4,3,1,0,2:T(8,128)(2,1)} collective-permute-done((bf16[4,2,3,2,64,128]{5,4,3,1,0,2:T(8,128)(2,1)}, bf16[4,2,3,2,64,128]{5,4,3,1,0,2:T(8,128)(2,1)}, u32[]{:S(2)}, u32[]{:S(2)}) %collective-permute-start.10) | collective-permute-done | bytes 786464 | tf_op jit(solution)/shard_map/ppermute | solution.py:78
  141.9 0.6 dynamic-slice
  142.5 0.8 dynamic-update-slice
  143.3 14.2 %all-reduce.3 = s32[8]{0:T(128)S(1)} all-reduce(s32[8]{0:T(128)S(1)} %dynamic-update-slice), channel_id=1, replica_groups=mesh['elec'=8,'space'=4] {'elec'}, use_global_device_ids=true, to_apply=%add.3 | all-reduce | flops 8 | bytes 64
  157.4 0.2 reduce-window.8
  157.6 30.8 %all_gather.6 = s32[8,48,4]{1,2,0:T(4,128)S(1)} all-gather(s32[1,48,4]{1,2,0:T(4,128)S(1)} %copy-done.2), channel_id=1, replica_groups=mesh['elec'=8,'space'=4] {'elec'}, dimensions={0}, use_global_device_ids=true | all-gather | bytes 6912 | tf_op jit(solution)/shard_map/all_gather | solution.py:84
  188.5 0.1 convert_reduce_fusion
  188.6 2.2 collective-permute-start.12
  190.8 0.1 copy.12
  191.0 0.7 gather_fusion
  191.7 0.6 gather_fusion.1
  192.2 0.2 slice_reduce_fusion.3
  192.5 0.1 subtract_convert_fusion
  192.5 11.3 %collective-permute-done.12 = bf16[4,2,3,2,64,128]{5,4,3,1,0,2:T(8,128)(2,1)} collective-permute-done((bf16[4,2,3,2,64,128]{5,4,3,1,0,2:T(8,128)(2,1)}, bf16[4,2,3,2,64,128]{5,4,3,1,0,2:T(8,128)(2,1)}, u32[]{:S(2)}, u32[]{:S(2)}) %collective-permute-start.12) | collective-permute-done | bytes 786464 | tf_op jit(solution)/shard_map/ppermute | solution.py:78
  203.8 2.3 constant_dynamic-update-slice_fusion.15
  206.1 2.2 constant_dynamic-update-slice_fusion.14
  208.3 2.2 constant_dynamic-update-slice_fusion.13
  210.6 2.3 constant_dynamic-update-slice_fusion.12
  212.8 1.1 constant_dynamic-update-slice_fusion.11
  213.9 1.1 constant_dynamic-update-slice_fusion.10
  214.9 1.1 constant_dynamic-update-slice_fusion.9
  216.0 1.1 constant_dynamic-update-slice_fusion.8
  217.1 2.3 constant_dynamic-update-slice_fusion.7
  219.4 2.3 constant_dynamic-update-slice_fusion.6
  221.6 2.3 constant_dynamic-update-slice_fusion.5
  223.9 2.2 constant_dynamic-update-slice_fusion.4
  226.1 1.0 constant_dynamic-update-slice_fusion.3
  227.2 1.0 constant_dynamic-update-slice_fusion.2
  228.2 1.0 constant_dynamic-update-slice_fusion.1
  229.2 1.1 constant_dynamic-update-slice_fusion
  230.3 4.3 %constant_dynamic-slice_fusion = bf16[32,2,3,2,64,128]{5,4,3,1,0,2:T(8,128)(2,1)S(1)} fusion(bf16[64,2,3,2,64,128]{5,4,3,1,0,2:T(8,128)(2,1)} %constant_dynamic-update-slice_fusion, s32[]{:T(128)S(6)} %select_n.52), kind=kLoop, calls=%fused_computation.118 | loop fusion | bytes 12582916 | tf_op jit(solution)/shard_map/jit(_roll_dynamic)/dynamic_slice | solution.py:79
  234.6 2.9 %copy.13 = bf16[32,2,3,2,64,128]{5,4,3,2,1,0:T(8,128)(2,1)S(1)} copy(bf16[32,2,3,2,64,128]{5,4,3,1,0,2:T(8,128)(2,1)S(1)} %constant_dynamic-slice_fusion) | data formatting | bytes 12582912 | tf_op jit(solution)/shard_map/jit(_roll_dynamic)/dynamic_slice | solution.py:79
  237.5 8.3 %fusion = f32[32,98304]{1,0:T(8,128)} fusion(bf16[4,8,768,128]{3,2,1,0:T(8,128)(2,1)S(1)} %bitcast.61, bf16[16,32]{1,0:T(8,128)(2,1)S(1)} %get-tuple-element.27, bf16[16,32]{1,0:T(8,128)(2,1)S(1)} %get-tuple-element.28), kind=kOutput, calls=%fused_computation.2 | convolution fusion | flops 201330688 | bytes 18876416 | tf_op jit(solution)/shard_map/dot_general | solution.py:103
  245.8 8.0 %slice_bitcast_fusion.1 = (f32[2,8,768,128]{3,1,2,0:T(8,128)}, f32[2,8,768,128]{3,1,2,0:T(8,128)S(1)}) fusion(f32[32,98304]{1,0:T(8,128)} %fusion), kind=kLoop, calls=%fused_computation.6 | loop fusion | bytes 25165824
  253.8 4.2 %copy.15 = f32[2,8,768,128]{3,2,1,0:T(8,128)S(1)} copy(f32[2,8,768,128]{3,1,2,0:T(8,128)} %get-tuple-element.11) | data formatting | bytes 12582912
  258.0 0.0 copy-start
  258.0 0.0 copy-start.1
  258.0 1.2 copy.16
  259.3 1.7 subtract_reduce_fusion
  261.0 0.4 fusion.5
  261.3 1.1 pad_maximum_fusion
  (26 shorter events, 0.1 us)
Async XLA Ops:
  0.0 141.9 %copy-start.3 = (u32[32]{0:T(128)S(1)}, u32[32]{0:T(128)}, u32[]{:S(2)}) copy-start(u32[32]{0:T(128)} %constant.87) | copy-start | bytes 388
  0.0 157.6 %copy-start.2 = (s32[1,48,4]{1,2,0:T(4,128)S(1)}, s32[1,48,4]{1,2,0:T(4,128)}, u32[]{:S(2)}) copy-start(s32[1,48,4]{1,2,0:T(4,128)} %param.11) | copy-start | bytes 2308
  1.1 6.4 %collective-permute-start = (f32[4,2,1,64,128]{4,3,2,1,0:T(8,128)S(1)}, f32[4,2,1,64,128]{4,3,2,1,0:T(8,128)S(1)}, u32[]{:S(2)}, u32[]{:S(2)}) collective-permute-start(f32[4,2,1,64,128]{4,3,2,1,0:T(8,128)S(1)} %get-tuple-element.21), channel_id=1, source_target_pairs={{1,0},{2,1},{3,2},{5,4},{6,5},{7,6},{9,8},{10,9},{11,10},{13,12},{... | collective-permute-start | bytes 786440 | tf_op jit(solution)/shard_map/ppermute | solution.py:23
  2.4 5.1 %collective-permute-start.1 = (f32[4,2,1,64,128]{4,3,2,1,0:T(8,128)S(1)}, f32[4,2,1,64,128]{4,3,2,1,0:T(8,128)S(1)}, u32[]{:S(2)}, u32[]{:S(2)}) collective-permute-start(f32[4,2,1,64,128]{4,3,2,1,0:T(8,128)S(1)} %get-tuple-element.22), channel_id=1, source_target_pairs={{0,1},{1,2},{2,3},{4,5},{5,6},{6,7},{8,9},{9,10},{10,11},{12,13},{... | collective-permute-start | bytes 786440 | tf_op jit(solution)/shard_map/ppermute | solution.py:21
  10.6 7.7 %collective-permute-start.2 = (f32[4,2,1,64,128]{4,3,2,1,0:T(8,128)S(1)}, f32[4,2,1,64,128]{4,3,2,1,0:T(8,128)S(1)}, u32[]{:S(2)}, u32[]{:S(2)}) collective-permute-start(f32[4,2,1,64,128]{4,3,2,1,0:T(8,128)S(1)} %get-tuple-element.19), channel_id=1, source_target_pairs={{1,0},{2,1},{3,2},{5,4},{6,5},{7,6},{9,8},{10,9},{11,10},{13,12},{... | collective-permute-start | bytes 786440 | tf_op jit(solution)/shard_map/ppermute | solution.py:23
  11.9 7.5 %collective-permute-start.3 = (f32[4,2,1,64,128]{4,3,2,1,0:T(8,128)S(1)}, f32[4,2,1,64,128]{4,3,2,1,0:T(8,128)S(1)}, u32[]{:S(2)}, u32[]{:S(2)}) collective-permute-start(f32[4,2,1,64,128]{4,3,2,1,0:T(8,128)S(1)} %get-tuple-element.20), channel_id=1, source_target_pairs={{0,1},{1,2},{2,3},{4,5},{5,6},{6,7},{8,9},{9,10},{10,11},{12,13},{... | collective-permute-start | bytes 786440 | tf_op jit(solution)/shard_map/ppermute | solution.py:21
  19.8 7.9 %collective-permute-start.4 = (bf16[4,2,1,64,128]{4,3,2,1,0:T(8,128)(2,1)S(1)}, bf16[4,2,1,64,128]{4,3,2,1,0:T(8,128)(2,1)S(1)}, u32[]{:S(2)}, u32[]{:S(2)}) collective-permute-start(bf16[4,2,1,64,128]{4,3,2,1,0:T(8,128)(2,1)S(1)} %get-tuple-element.23), channel_id=1, source_target_pairs={{0,1},{1,2},{2,3},{4,5},{5,6},{6,7},{8,9},{9,10},{10,11},{12,13},{... | collective-permute-start | bytes 393224 | tf_op jit(solution)/shard_map/ppermute | solution.py:21
  26.4 5.2 %collective-permute-start.5 = (bf16[4,2,1,64,128]{4,3,2,1,0:T(8,128)(2,1)S(1)}, bf16[4,2,1,64,128]{4,3,2,1,0:T(8,128)(2,1)S(1)}, u32[]{:S(2)}, u32[]{:S(2)}) collective-permute-start(bf16[4,2,1,64,128]{4,3,2,1,0:T(8,128)(2,1)S(1)} %get-tuple-element.24), channel_id=1, source_target_pairs={{1,0},{2,1},{3,2},{5,4},{6,5},{7,6},{9,8},{10,9},{11,10},{13,12},{... | collective-permute-start | bytes 393224 | tf_op jit(solution)/shard_map/ppermute | solution.py:23
  32.3 20.4 %collective-permute-start.6 = (bf16[4,2,3,2,64,128]{5,4,3,1,0,2:T(8,128)(2,1)S(1)}, bf16[4,2,3,2,64,128]{5,4,3,1,0,2:T(8,128)(2,1)S(1)}, u32[]{:S(2)}, u32[]{:S(2)}) collective-permute-start(bf16[4,2,3,2,64,128]{5,4,3,1,0,2:T(8,128)(2,1)S(1)} %pad_maximum_fusion.1), channel_id=1, source_target_pairs={{0,4},{4,8},{8,12},{12,16},{16,20},{20,24},{24,28},{28,0},{1,5},{5... | collective-permute-start | bytes 2359304 | tf_op jit(solution)/shard_map/ppermute | solution.py:78
  52.7 21.4 %collective-permute-start.7 = (bf16[4,2,3,2,64,128]{5,4,3,1,0,2:T(8,128)(2,1)S(1)}, bf16[4,2,3,2,64,128]{5,4,3,1,0,2:T(8,128)(2,1)S(1)}, u32[]{:S(2)}, u32[]{:S(2)}) collective-permute-start(bf16[4,2,3,2,64,128]{5,4,3,1,0,2:T(8,128)(2,1)S(1)} %collective-permute-done.6), channel_id=1, source_target_pairs={{0,4},{4,8},{8,12},{12,16},{16,20},{20,24},{24,28},{28,0},{1,5},{5... | collective-permute-start | bytes 2359304 | tf_op jit(solution)/shard_map/ppermute | solution.py:78
  74.2 22.6 %collective-permute-start.8 = (bf16[4,2,3,2,64,128]{5,4,3,1,0,2:T(8,128)(2,1)S(1)}, bf16[4,2,3,2,64,128]{5,4,3,1,0,2:T(8,128)(2,1)S(1)}, u32[]{:S(2)}, u32[]{:S(2)}) collective-permute-start(bf16[4,2,3,2,64,128]{5,4,3,1,0,2:T(8,128)(2,1)S(1)} %collective-permute-done.7), channel_id=1, source_target_pairs={{0,4},{4,8},{8,12},{12,16},{16,20},{20,24},{24,28},{28,0},{1,5},{5... | collective-permute-start | bytes 2359304 | tf_op jit(solution)/shard_map/ppermute | solution.py:78
  96.8 22.5 %collective-permute-start.9 = (bf16[4,2,3,2,64,128]{5,4,3,1,0,2:T(8,128)(2,1)S(1)}, bf16[4,2,3,2,64,128]{5,4,3,1,0,2:T(8,128)(2,1)}, u32[]{:S(2)}, u32[]{:S(2)}) collective-permute-start(bf16[4,2,3,2,64,128]{5,4,3,1,0,2:T(8,128)(2,1)S(1)} %collective-permute-done.8), channel_id=1, source_target_pairs={{0,4},{4,8},{8,12},{12,16},{16,20},{20,24},{24,28},{28,0},{1,5},{5... | collective-permute-start | bytes 2359304 | tf_op jit(solution)/shard_map/ppermute | solution.py:78
  119.3 21.9 %collective-permute-start.10 = (bf16[4,2,3,2,64,128]{5,4,3,1,0,2:T(8,128)(2,1)}, bf16[4,2,3,2,64,128]{5,4,3,1,0,2:T(8,128)(2,1)}, u32[]{:S(2)}, u32[]{:S(2)}) collective-permute-start(bf16[4,2,3,2,64,128]{5,4,3,1,0,2:T(8,128)(2,1)} %collective-permute-done.9), channel_id=1, source_target_pairs={{0,4},{4,8},{8,12},{12,16},{16,20},{20,24},{24,28},{28,0},{1,5},{5... | collective-permute-start | bytes 2359304 | tf_op jit(solution)/shard_map/ppermute | solution.py:78
  141.3 47.3 %collective-permute-start.11 = (bf16[4,2,3,2,64,128]{5,4,3,1,0,2:T(8,128)(2,1)}, bf16[4,2,3,2,64,128]{5,4,3,1,0,2:T(8,128)(2,1)}, u32[]{:S(2)}, u32[]{:S(2)}) collective-permute-start(bf16[4,2,3,2,64,128]{5,4,3,1,0,2:T(8,128)(2,1)} %collective-permute-done.10), channel_id=1, source_target_pairs={{0,4},{4,8},{8,12},{12,16},{16,20},{20,24},{24,28},{28,0},{1,5},{5... | collective-permute-start | bytes 2359304 | tf_op jit(solution)/shard_map/ppermute | solution.py:78
  188.6 15.2 %collective-permute-start.12 = (bf16[4,2,3,2,64,128]{5,4,3,1,0,2:T(8,128)(2,1)}, bf16[4,2,3,2,64,128]{5,4,3,1,0,2:T(8,128)(2,1)}, u32[]{:S(2)}, u32[]{:S(2)}) collective-permute-start(bf16[4,2,3,2,64,128]{5,4,3,1,0,2:T(8,128)(2,1)} %collective-permute-done.11), channel_id=1, source_target_pairs={{0,4},{4,8},{8,12},{12,16},{16,20},{20,24},{24,28},{28,0},{1,5},{5... | collective-permute-start | bytes 2359304 | tf_op jit(solution)/shard_map/ppermute | solution.py:78
  258.0 2.9 %copy-start = (f32[2,64,128]{2,1,0:T(8,128)S(1)}, f32[2,64,128]{2,1,0:T(8,128)}, u32[]{:S(2)}) copy-start(f32[2,64,128]{2,1,0:T(8,128)} %param.7) | copy-start | bytes 196612
  258.0 2.9 %copy-start.1 = (f32[2,64,128]{2,1,0:T(8,128)S(1)}, f32[2,64,128]{2,1,0:T(8,128)}, u32[]{:S(2)}) copy-start(f32[2,64,128]{2,1,0:T(8,128)} %param.6) | copy-start | bytes 196612
